TPU v7x, 32 devices: a whole 2x2x4 slice. The times are simulated.
32 devices in a mesh: win: 16 (over z, y, x), rcv: 2 (over core).
Axes of the slice: x: 2, y: 2, z: 4, core: 2. Of those that a mesh axis runs over, the one named last changes fastest.
Arguments:
- spectra: bfloat16 [32, 2, 32, 4096], P('win', None, 'rcv'), may hold values from -6 to 6
- source_channel: int32 [8], replicated, may hold values from 0 to 31
Outputs:
- stack: float32 [512, 8, 32], P('win', None, 'rcv')
All inputs are finite; a program needn't handle non-finite values.
Results may differ from a plain program's by a relative error of at most 0.0011.
Values may be sent and summed in bfloat16 or wider, within the bound.
No kernel may reach another device: no remote copies, remote signals or barrier semaphores. Data moves between devices by JAX's collectives and lax.ppermute only.
A program may use at most 64 MiB of HBM per device.

v0:
```python
import jax
import jax.numpy as jnp
from jax import lax
from jax.sharding import PartitionSpec as P

L = 512
ITERS = 5


TUKEY = 4.685
EPSILON = 1e-06


def make_basis(bin_count, lag_count):
    freq = jnp.arange(bin_count, dtype=jnp.int32)
    shifts = jnp.arange(lag_count, dtype=jnp.int32) - lag_count // 2
    phase = shifts[:, None] * freq[None, :] % (2 * bin_count)
    angle = phase.astype(jnp.float32) * (2.0 * jnp.pi / (2 * bin_count))
    factor = jnp.where(freq == 0, 1.0, 2.0).astype(jnp.float32) / jnp.sqrt(
        jnp.float32(8 * bin_count)
    )
    table = jnp.concatenate(
        [jnp.cos(angle) * factor[None, :], -jnp.sin(angle) * factor[None, :]], axis=1
    )
    return table.astype(jnp.bfloat16)


def bisquare_stack(samples):
    center = jnp.mean(samples, axis=0)
    for iteration in range(ITERS):
        deviation = samples - center
        squared = deviation * deviation
        scale_two = jnp.mean(squared, axis=0) + EPSILON
        ratio = squared / (TUKEY * TUKEY * scale_two)
        weight = jnp.where(ratio < 1.0, (1.0 - ratio) * (1.0 - ratio), 0.0)
        center = jnp.sum(weight * samples, axis=0) / jnp.sum(weight, axis=0)
    return center


def per_device(spectra, source_channel):
    win_count = spectra.shape[0]
    chan_count = spectra.shape[2]
    bin_count = spectra.shape[3]
    source_count = source_channel.shape[0]
    whole = lax.all_gather(spectra, "rcv", axis=2, tiled=True)
    channels = lax.iota(jnp.int32, whole.shape[2])
    onehot = (source_channel[:, None] == channels[None, :]).astype(jnp.bfloat16)
    picked = jnp.einsum("sr,wcrf->wcsf", onehot, whole, preferred_element_type=jnp.float32).astype(
        jnp.bfloat16
    )
    source_float = picked.astype(jnp.float32)
    receiver_float = spectra.astype(jnp.float32)
    real_a = source_float[:, 0][:, :, None, :]
    imag_b = source_float[:, 1][:, :, None, :]
    real_p = receiver_float[:, 0][:, None, :, :]
    imag_q = receiver_float[:, 1][:, None, :, :]
    pair_count = source_count * chan_count
    real_part = (real_a * real_p + imag_b * imag_q).reshape(win_count, pair_count, bin_count)
    imag_part = (imag_b * real_p - real_a * imag_q).reshape(win_count, pair_count, bin_count)
    cross = jnp.concatenate([real_part, imag_part], axis=2).astype(jnp.bfloat16)
    basis = make_basis(bin_count, L)
    corr = jnp.einsum("lk,wpk->wlp", basis, cross, preferred_element_type=jnp.float32)
    block = L // lax.axis_size("win")
    regrouped = lax.all_to_all(corr, "win", split_axis=1, concat_axis=0, tiled=True)
    result = bisquare_stack(regrouped)
    return result.reshape(block, source_count, chan_count)


def solution(mesh):
    return jax.shard_map(
        per_device,
        mesh=mesh,
        in_specs=(P("win", None, "rcv", None), P()),
        out_specs=P("win", None, "rcv"),
        check_vma=False,
    )
```

profile of v0, /device:TPU:0, one launch (start us, length us, event | category | flops | bytes accessed | tf_op | source)
XLA Modules:
  0.0 82.3 jit_solution(5158655815542492971)
XLA Ops:
  6.5 0.0 all-gather.2.cloned.1.call-start
  6.5 0.7 all-gather.2.cloned.1.call-update
  7.3 0.0 copy-start.2
  7.3 0.0 copy-start.3
  7.3 36.0 %multiply_convert_fusion.1 = (bf16[512,4096]{1,0:T(8,128)(2,1)}, bf16[512,4096]{1,0:T(8,128)(2,1)}) fusion(f32[4096]{0:T(1024)S(1)} %select_multiply_fusion, s32[512]{0:T(512)S(1)} %iota_add_fusion), kind=kLoop, calls=%fused_computation.11 | loop fusion | flops 39845888 | bytes 8407040 | tf_op jit(solution)/shard_map/convert.1
  43.3 0.0 copy-done.2
  43.3 0.1 convert_element_type.24
  43.4 0.1 slice_bitcast_fusion.1
  43.5 0.0 all-gather.2.cloned.1.call-done
  43.5 0.0 copy-done.3
  43.5 0.0 copy-start
  43.5 0.0 copy-start.1
  43.5 1.7 %fusion.10 = f32[2,2,8,4096]{3,2,1,0:T(8,128)S(1)} fusion(bf16[2,2,32,4096]{3,2,1,0:T(8,128)(2,1)} %all-gather.2.cloned.1.call-done, s32[8]{0:T(128)S(1)} %copy-done.3), kind=kOutput, calls=%fused_computation.17 | convolution fusion | flops 8651008 | bytes 1572896 | tf_op jit(solution)/shard_map/sr,wcrf->wcsf/dot_general | solution.py:48
  45.2 1.2 %add_convert_fusion = (bf16[2,8,16,4096]{3,2,1,0:T(8,128)(2,1)S(1)}, bf16[2,8,16,4096]{3,2,1,0:T(8,128)(2,1)S(1)}) fusion(f32[2,16,4096]{2,1,0:T(8,128)S(1)} %get-tuple-element.18, f32[2,8,4096]{2,1,0:T(8,128)S(1)} %get-tuple-element.20, f32[2,16,4096]{2,1,0:T(8,128)S(1)} %get-tuple-element.17, f32[2,8,4096]{2,1,0:T(8,128)S(1)} %get-tuple-element.19), kind=kLoop, calls=%fused_computation.22 | loop fusion | flops 8388608 | bytes 5767168 | tf_op jit(solution)/shard_map/convert.6
  46.4 0.0 copy-done
  46.4 0.8 %copy-done.1 = bf16[512,4096]{1,0:T(8,128)(2,1)S(1)} copy-done((bf16[512,4096]{1,0:T(8,128)(2,1)S(1)}, bf16[512,4096]{1,0:T(8,128)(2,1)}, u32[]{:S(2)}) %copy-start.1) | copy-done | bytes 4194328
  47.3 2.4 %fusion.14 = f32[2,512,128]{1,2,0:T(8,128)S(1)} fusion(bf16[512,4096]{1,0:T(8,128)(2,1)S(1)} %copy-done.1, bf16[512,4096]{1,0:T(8,128)(2,1)S(1)} %copy-done, bf16[2,128,4096]{2,1,0:T(8,128)(2,1)S(1)} %bitcast.41, bf16[2,128,4096]{2,1,0:T(8,128)(2,1)S(1)} %bitcast.40), kind=kOutput, calls=%fused_computation.23 | convolution fusion | flops 2172649472 | bytes 13107200 | tf_op jit(solution)/shard_map/lk,wpk->wlp/dot_general | solution.py:62
  49.6 0.2 copy.7
  49.9 23.3 %all_to_all.15 = f32[2,512,128]{2,0,1:T(2,128)S(1)} all-to-all(f32[2,512,128]{2,0,1:T(2,128)S(1)} %copy.7), channel_id=1, replica_groups=mesh['win'=16,'rcv'=2] {'win'}, dimensions={1} | all-to-all | bytes 1048576 | tf_op jit(solution)/shard_map/all_to_all | solution.py:64
  73.2 0.1 fusion.17
  73.3 0.2 fusion.22
  73.5 0.1 fusion.18
  73.6 0.2 fusion.23
  73.8 0.1 fusion.19
  73.9 0.2 fusion.24
  74.1 0.1 fusion.20
  74.2 0.2 fusion.25
  74.4 0.1 fusion.21
  74.5 0.2 fusion.26
  74.7 0.7 copy.9
  (16 shorter events, 0.2 us)
Async XLA Ops:
  6.5 36.9 %all-gather.2.cloned.1.call-start = ((), (), s32[]{:S(2)}) async-start(), calls=%async_computation.1 | async-start | bytes 1572864 | tf_op jit(solution)/shard_map/all_gather | solution.py:45
  7.3 36.0 %copy-start.2 = (bf16[2,2,16,4096]{3,2,1,0:T(8,128)(2,1)S(1)}, bf16[2,2,16,4096]{3,2,1,0:T(8,128)(2,1)}, u32[]{:S(2)}) copy-start(bf16[2,2,16,4096]{3,2,1,0:T(8,128)(2,1)} %param.2) | copy-start | bytes 1572868
  7.3 36.2 %copy-start.3 = (s32[8]{0:T(128)S(1)}, s32[8]{0:T(128)}, u32[]{:S(2)}) copy-start(s32[8]{0:T(128)} %param.3) | copy-start | bytes 100
  43.5 2.9 %copy-start = (bf16[512,4096]{1,0:T(8,128)(2,1)S(1)}, bf16[512,4096]{1,0:T(8,128)(2,1)}, u32[]{:S(2)}) copy-start(bf16[512,4096]{1,0:T(8,128)(2,1)} %get-tuple-element.21) | copy-start | bytes 12582916
  43.5 3.8 %copy-start.1 = (bf16[512,4096]{1,0:T(8,128)(2,1)S(1)}, bf16[512,4096]{1,0:T(8,128)(2,1)}, u32[]{:S(2)}) copy-start(bf16[512,4096]{1,0:T(8,128)(2,1)} %get-tuple-element.22) | copy-start | bytes 12582916
Sparse Core Ops, SparseCore 0:
  8.9 11.7 all-gather.1
where the time goes:
time: 82.4 us; the launch traced here: 82.3 us
  other arithmetic  38.6 us (47%)
  blocking collectives  23.3 us (28%)
  between operations  13.6 us (17%)
  matrix products  4.04 us (5%)
  local copies, waits for them, and re-layouts  1.96 us (2%)
    another operation x2, other arithmetic  37.2 us
    all_to_all x1, blocking collectives, per_device(): lax.all_to_all(corr, 'win', split_axis=1, concat_axis=0, tiled=True)  23.3 us
    dot_general x1, matrix products, per_device(): jnp.einsum('lk,wpk->wlp', basis, cross, preferred_element_type=jnp.float32)  2.36 us
    dot_general x1, matrix products, per_device(): jnp.einsum('sr,wcrf->wcsf', onehot, whole, preferred_element_type=jnp.flo...  1.69 us
  transfers between devices with their start and end apart: 1, of which 0 were waited for; matrix products, arithmetic and copies ran while one was open for 44% of the time, Pallas kernels for 0%

commit v1 on v0

v1 whole, which is shorter than its diff:
```python
import jax
import jax.numpy as jnp
import numpy as np
from jax import lax
from jax.sharding import PartitionSpec as P

L = 512
ITERS = 5


TUKEY = 4.685
EPSILON = 1e-06


def make_basis(bin_count, lag_count):
    freq = np.arange(bin_count, dtype=np.int64)
    shifts = np.arange(lag_count, dtype=np.int64) - lag_count // 2
    phase = shifts[:, None] * freq[None, :] % (2 * bin_count)
    angle = phase * (2.0 * np.pi / (2 * bin_count))
    factor = np.where(freq == 0, 1.0, 2.0) / np.sqrt(8.0 * bin_count)
    table = np.concatenate([np.cos(angle) * factor[None, :], -np.sin(angle) * factor[None, :]], axis=1)
    return jnp.asarray(table.astype(np.float32).astype(jnp.bfloat16))


def bisquare_stack(samples):
    center = jnp.mean(samples, axis=0)
    for iteration in range(ITERS):
        deviation = samples - center
        squared = deviation * deviation
        scale_two = jnp.mean(squared, axis=0) + EPSILON
        ratio = squared / (TUKEY * TUKEY * scale_two)
        weight = jnp.where(ratio < 1.0, (1.0 - ratio) * (1.0 - ratio), 0.0)
        center = jnp.sum(weight * samples, axis=0) / jnp.sum(weight, axis=0)
    return center


def per_device(spectra, source_channel):
    win_count = spectra.shape[0]
    chan_count = spectra.shape[2]
    bin_count = spectra.shape[3]
    source_count = source_channel.shape[0]
    receivers_parts = lax.axis_size("rcv")
    channels = lax.iota(jnp.int32, chan_count) + lax.axis_index("rcv") * chan_count
    onehot = (source_channel[:, None] == channels[None, :]).astype(jnp.bfloat16)
    own = jnp.einsum("sr,wcrf->wcsf", onehot, spectra, preferred_element_type=jnp.float32).astype(
        jnp.bfloat16
    )
    picked = own
    moving = own
    for step in range(receivers_parts - 1):
        moving = lax.ppermute(
            moving, "rcv", [(i, (i + 1) % receivers_parts) for i in range(receivers_parts)]
        )
        picked = picked + moving
    source_float = picked.astype(jnp.float32)
    receiver_float = spectra.astype(jnp.float32)
    real_a = source_float[:, 0][:, :, None, :]
    imag_b = source_float[:, 1][:, :, None, :]
    real_p = receiver_float[:, 0][:, None, :, :]
    imag_q = receiver_float[:, 1][:, None, :, :]
    pair_count = source_count * chan_count
    real_part = (real_a * real_p + imag_b * imag_q).reshape(win_count, pair_count, bin_count)
    imag_part = (imag_b * real_p - real_a * imag_q).reshape(win_count, pair_count, bin_count)
    cross = jnp.concatenate([real_part, imag_part], axis=2).astype(jnp.bfloat16)
    basis = make_basis(bin_count, L)
    corr = jnp.einsum("lk,wpk->lwp", basis, cross, preferred_element_type=jnp.float32)
    parts = lax.axis_size("win")
    block = L // parts
    corr = corr.astype(jnp.bfloat16).reshape(parts, block, win_count * pair_count)
    regrouped = lax.all_to_all(corr, "win", split_axis=0, concat_axis=0, tiled=True)
    regrouped = regrouped.reshape(parts, block, win_count, pair_count).astype(jnp.float32)
    regrouped = regrouped.transpose(0, 2, 1, 3).reshape(parts * win_count, block, pair_count)
    result = bisquare_stack(regrouped)
    return result.reshape(block, source_count, chan_count)


def solution(mesh):
    return jax.shard_map(
        per_device,
        mesh=mesh,
        in_specs=(P("win", None, "rcv", None), P()),
        out_specs=P("win", None, "rcv"),
        check_vma=False,
    )
```

time: 82.4 us -> 34.8 us (0.42)
  other arithmetic: 38.6 us -> 8.44 us
  between operations: 13.6 us -> 0.25 us
  blocking collectives: 23.3 us -> 18.2 us
  local copies, waits for them, and re-layouts: 1.96 us -> 3.43 us
    another operation x2 -> x1, other arithmetic: 37.2 us -> 1.18 us
    all_to_all x1, blocking collectives: 23.3 us -> 18.2 us  [per_device(): lax.all_to_all(corr, 'win', split_axis=0, concat_axis=0, tiled=True)]
    reduce_sum x5, other arithmetic: 0.9 us -> 4.37 us  [bisquare_stack(): center = jnp.sum(weight * samples, axis=0) / jnp.sum(weight, axis=0)]
    reduce_sum x5, other arithmetic: 0.37 us -> 1.53 us  [bisquare_stack(): scale_two = jnp.mean(squared, axis=0) + EPSILON]
    unnamed x8 -> x2, local copies, waits for them, and re-layouts: 0.86 us -> 2.01 us
    convert_element_type x1, other arithmetic: 0.07 us -> 1.11 us  [per_device(): receiver_float = spectra.astype(jnp.float32)]
  transfers between devices with their start and end apart: 1 -> 1, of which waited for: 0 -> 0; matrix products, arithmetic and copies ran while one was open for 44% -> 3% of each run, Pallas kernels for 0% -> 0%
where the time goes in v1:
time: 34.8 us; the launch traced here: 34.5 us
  blocking collectives  18.2 us (52%)
  other arithmetic  8.44 us (24%)
  matrix products  3.69 us (11%)
  local copies, waits for them, and re-layouts  3.43 us (10%)
  starting transfers between devices  0.52 us (1%)
    all_to_all x1, blocking collectives, per_device(): lax.all_to_all(corr, 'win', split_axis=0, concat_axis=0, tiled=True)  18.2 us
    reduce_sum x5, other arithmetic, bisquare_stack(): center = jnp.sum(weight * samples, axis=0) / jnp.sum(weight, axis=0)  4.37 us
    dot_general x1, matrix products, per_device(): jnp.einsum('lk,wpk->lwp', basis, cross, preferred_element_type=jnp.float32)  2.36 us
    unnamed x2, local copies, waits for them, and re-layouts  2.01 us
    reduce_sum x5, other arithmetic, bisquare_stack(): scale_two = jnp.mean(squared, axis=0) + EPSILON  1.53 us
    dot_general x1, matrix products, per_device(): jnp.einsum('sr,wcrf->wcsf', onehot, spectra, preferred_element_type=jnp.f...  1.33 us
    another operation x1, other arithmetic  1.18 us
    convert_element_type x1, other arithmetic, per_device(): receiver_float = spectra.astype(jnp.float32)  1.11 us
  transfers between devices with their start and end apart: 1, of which 0 were waited for; matrix products, arithmetic and copies ran while one was open for 3% of the time, Pallas kernels for 0%

profile of v1, /device:TPU:0, one launch (start us, length us, event | category | flops | bytes accessed | tf_op | source)
XLA Modules:
  0.0 34.5 jit_solution(17217073171922386818)
XLA Ops:
  0.0 1.3 %fusion = bf16[2,2,8,4096]{3,2,1,0:T(8,128)(2,1)S(1)} fusion(bf16[2,2,16,4096]{3,2,1,0:T(8,128)(2,1)} %param.3, s32[16]{0:T(128)S(1)} %iota_add_fusion, s32[8]{0:T(128)} %param.4), kind=kOutput, calls=%fused_computation.1 | convolution fusion | flops 4325504 | bytes 786528 | tf_op jit(solution)/shard_map/sr,wcrf->wcsf/dot_general | solution.py:45
  1.3 0.5 %collective-permute-start = (bf16[2,2,8,4096]{3,2,1,0:T(8,128)(2,1)S(1)}, bf16[2,2,8,4096]{3,2,1,0:T(8,128)(2,1)S(1)}, u32[]{:S(2)}, u32[]{:S(2)}) collective-permute-start(bf16[2,2,8,4096]{3,2,1,0:T(8,128)(2,1)S(1)} %fusion), channel_id=1, source_target_pairs={{0,1},{1,0},{2,3},{3,2},{4,5},{5,4},{6,7},{7,6},{8,9},{9,8},{10,11... | collective-permute-start | bytes 786440 | tf_op jit(solution)/shard_map/ppermute | solution.py:51
  1.9 1.1 %convert_element_type.27 = f32[2,2,16,4096]{3,2,1,0:T(8,128)S(1)} convert(bf16[2,2,16,4096]{3,2,1,0:T(8,128)(2,1)} %param.3) | non-fusion elementwise | flops 262144 | bytes 1572864 | tf_op jit(solution)/shard_map/convert_element_type | solution.py:56
  3.0 0.0 copy-start
  3.0 0.1 slice_bitcast_fusion.1
  3.1 0.0 collective-permute-done
  3.2 1.2 %add_convert_fusion = (bf16[2,8,16,4096]{3,2,1,0:T(8,128)(2,1)S(1)}, bf16[2,8,16,4096]{3,2,1,0:T(8,128)(2,1)S(1)}) fusion(f32[2,16,4096]{2,1,0:T(8,128)S(1)} %get-tuple-element.18, f32[2,8,4096]{2,1,0:T(8,128)S(1)} %get-tuple-element.20, f32[2,16,4096]{2,1,0:T(8,128)S(1)} %get-tuple-element.17, f32[2,8,4096]{2,1,0:T(8,128)S(1)} %get-tuple-element.19), kind=kLoop, calls=%fused_computation.4 | loop fusion | flops 8388608 | bytes 5767168 | tf_op jit(solution)/shard_map/convert.5
  4.3 2.0 %copy-done = bf16[512,8192,1]{1,0,2:T(8,128)(2,1)S(1)} copy-done((bf16[512,8192,1]{1,0,2:T(8,128)(2,1)S(1)}, bf16[512,8192,1]{1,0,2:T(8,128)(2,1)}, u32[]{:S(2)}) %copy-start) | copy-done | bytes 8388632
  6.4 2.4 %fusion.3 = bf16[512,2,128]{0,2,1:T(8,128)(2,1)S(1)} fusion(bf16[512,8192,1]{1,0,2:T(8,128)(2,1)S(1)} %copy-done, bf16[2,128,4096]{2,1,0:T(8,128)(2,1)S(1)} %bitcast.76, bf16[2,128,4096]{2,1,0:T(8,128)(2,1)S(1)} %bitcast.75), kind=kOutput, calls=%fused_computation.7 | convolution fusion | flops 2156003328 | bytes 12845056 | tf_op jit(solution)/shard_map/lk,wpk->lwp/dot_general | solution.py:66
  8.7 0.2 copy.7
  8.9 0.2 reshape.84
  9.1 18.2 %all_to_all.5 = bf16[16,32,256]{2,1,0:T(8,128)(2,1)S(1)} all-to-all(bf16[16,32,256]{2,1,0:T(8,128)(2,1)S(1)} %reshape.84), channel_id=1, replica_groups=mesh['win'=16,'rcv'=2] {'win'}, dimensions={0} | all-to-all | bytes 524288 | tf_op jit(solution)/shard_map/all_to_all | solution.py:70
  27.3 0.3 reshape.85
  27.5 0.1 bitcast_reduce_fusion
  27.7 0.3 fusion.18
  28.0 0.9 %fusion.28 = (f32[32,128]{1,0:T(8,128)S(1)}, f32[32,128]{1,0:T(8,128)S(1)}) fusion(f32[16,32,2,128]{3,2,1,0:T(2,128)S(1)} %reshape.85, f32[32,128]{1,0:T(8,128)S(1)} %add_multiply_fusion.4, f32[32,128]{1,0:T(8,128)S(1)} %broadcast_multiply_fusion), kind=kLoop, calls=%fused_computation.60 | loop fusion | flops 1302528 | bytes 589824 | tf_op jit(solution)/shard_map/reduce_sum | solution.py:33
  28.9 0.3 fusion.17
  29.2 0.9 %fusion.27 = (f32[32,128]{1,0:T(8,128)S(1)}, f32[32,128]{1,0:T(8,128)S(1)}) fusion(f32[16,32,2,128]{3,2,1,0:T(2,128)S(1)} %reshape.85, f32[32,128]{1,0:T(8,128)S(1)} %add_multiply_fusion.3, f32[32,128]{1,0:T(8,128)S(1)} %div.107), kind=kLoop, calls=%fused_computation.59 | loop fusion | flops 1302528 | bytes 589824 | tf_op jit(solution)/shard_map/reduce_sum | solution.py:33
  30.1 0.3 fusion.16
  30.4 0.9 %fusion.26 = (f32[32,128]{1,0:T(8,128)S(1)}, f32[32,128]{1,0:T(8,128)S(1)}) fusion(f32[16,32,2,128]{3,2,1,0:T(2,128)S(1)} %reshape.85, f32[32,128]{1,0:T(8,128)S(1)} %add_multiply_fusion.2, f32[32,128]{1,0:T(8,128)S(1)} %div.111), kind=kLoop, calls=%fused_computation.58 | loop fusion | flops 1302528 | bytes 589824 | tf_op jit(solution)/shard_map/reduce_sum | solution.py:33
  31.3 0.3 fusion.15
  31.7 0.9 %fusion.25 = (f32[32,128]{1,0:T(8,128)S(1)}, f32[32,128]{1,0:T(8,128)S(1)}) fusion(f32[16,32,2,128]{3,2,1,0:T(2,128)S(1)} %reshape.85, f32[32,128]{1,0:T(8,128)S(1)} %add_multiply_fusion.1, f32[32,128]{1,0:T(8,128)S(1)} %div.115), kind=kLoop, calls=%fused_computation.57 | loop fusion | flops 1302528 | bytes 589824 | tf_op jit(solution)/shard_map/reduce_sum | solution.py:33
  32.6 0.3 fusion.14
  32.9 0.9 %fusion.24 = (f32[32,128]{1,0:T(8,128)S(1)}, f32[32,128]{1,0:T(8,128)S(1)}) fusion(f32[16,32,2,128]{3,2,1,0:T(2,128)S(1)} %reshape.85, f32[32,128]{1,0:T(8,128)S(1)} %add_multiply_fusion, f32[32,128]{1,0:T(8,128)S(1)} %div.119), kind=kLoop, calls=%fused_computation.56 | loop fusion | flops 1302528 | bytes 589824 | tf_op jit(solution)/shard_map/reduce_sum | solution.py:33
  33.8 0.7 %copy.8 = f32[32,128]{0,1:T(8,128)} copy(f32[32,128]{1,0:T(8,128)S(1)} %div.123) | data formatting | bytes 32768 | tf_op jit(solution)/shard_map/div | solution.py:33
  (14 shorter events, 0.2 us)
Async XLA Ops:
  1.3 1.7 %collective-permute-start = (bf16[2,2,8,4096]{3,2,1,0:T(8,128)(2,1)S(1)}, bf16[2,2,8,4096]{3,2,1,0:T(8,128)(2,1)S(1)}, u32[]{:S(2)}, u32[]{:S(2)}) collective-permute-start(bf16[2,2,8,4096]{3,2,1,0:T(8,128)(2,1)S(1)} %fusion), channel_id=1, source_target_pairs={{0,1},{1,0},{2,3},{3,2},{4,5},{5,4},{6,7},{7,6},{8,9},{9,8},{10,11... | collective-permute-start | bytes 786440 | tf_op jit(solution)/shard_map/ppermute | solution.py:51
  3.0 3.4 %copy-start = (bf16[512,8192,1]{1,0,2:T(8,128)(2,1)S(1)}, bf16[512,8192,1]{1,0,2:T(8,128)(2,1)}, u32[]{:S(2)}) copy-start(bf16[512,8192,1]{1,0,2:T(8,128)(2,1)} %constant.26) | copy-start | bytes 25165828
